TPU v7x, 32 devices: a whole 2x2x4 slice. The times are simulated.
32 devices in a mesh: dp: 4 (over x, core), fsdp: 8 (over z, y).
Axes of the slice: x: 2, y: 2, z: 4, core: 2. Of those that a mesh axis runs over, the one named last changes fastest.
Arguments:
- query: bfloat16 [32768, 768], P(('dp', 'fsdp')), may hold values from -6 to 6
- memory: bfloat16 [32768, 768], P(('dp', 'fsdp')), may hold values from -6 to 6
- query_seg: int32 [32768], P(('dp', 'fsdp')), may hold values from 0 to 127, as said below
- memory_seg: int32 [32768], P(('dp', 'fsdp')), may hold values from 0 to 127, as said below
- attn_proj: bfloat16 [6, 768, 768], P(None, ('dp', 'fsdp')), may hold values from -0.21875 to 0.21875
- attn_out: bfloat16 [2, 768, 768], P(None, ('dp', 'fsdp')), may hold values from -3.5 to 3.5
- attn_bias: bfloat16 [6, 768], P(None, ('dp', 'fsdp')), may hold values from -3 to 3
- norm_gain: bfloat16 [3, 768], P(None, ('dp', 'fsdp')), may hold values from 0.25 to 1.75
- norm_bias: bfloat16 [3, 768], P(None, ('dp', 'fsdp')), may hold values from -2 to 2
- ffn_in: bfloat16 [768, 3072], P(('dp', 'fsdp')), may hold values from -0.21875 to 0.21875
- ffn_in_bias: bfloat16 [3072], P(('dp', 'fsdp')), may hold values from -3 to 3
- ffn_out: bfloat16 [3072, 768], P(('dp', 'fsdp')), may hold values from -0.109375 to 0.109375
- ffn_out_bias: bfloat16 [768], P(('dp', 'fsdp')), may hold values from -2 to 2
- cotangent: bfloat16 [32768, 768], P(('dp', 'fsdp')), may hold values from -6 to 6
Outputs:
- mixed: bfloat16 [32768, 768], P(('dp', 'fsdp'))
- query_grad: float32 [32768, 768], P(('dp', 'fsdp'))
- memory_grad: float32 [32768, 768], P(('dp', 'fsdp'))
- attn_proj_grad: float32 [6, 768, 768], P(None, ('dp', 'fsdp'))
- attn_out_grad: float32 [2, 768, 768], P(None, ('dp', 'fsdp'))
- attn_bias_grad: float32 [6, 768], P(None, ('dp', 'fsdp'))
- norm_gain_grad: float32 [3, 768], P(None, ('dp', 'fsdp'))
- norm_bias_grad: float32 [3, 768], P(None, ('dp', 'fsdp'))
- ffn_in_grad: float32 [768, 3072], P(('dp', 'fsdp'))
- ffn_in_bias_grad: float32 [3072], P(('dp', 'fsdp'))
- ffn_out_grad: float32 [3072, 768], P(('dp', 'fsdp'))
- ffn_out_bias_grad: float32 [768], P(('dp', 'fsdp'))
Inputs may be any that keep to these rules, and one draw needn't show every extreme that they name: `query_seg`: every aligned block of 512 query rows holds whole sequences, and the memory rows of the same block hold the same sequence numbers: block b carries either the single number b * 2 or the numbers b * 2 to b * 2 + 1 in rising runs, each run nonempty; the first block holds one sequence, the last holds 2. `memory_seg`: laid out as query_seg, block by block, with the same numbers in each block as query_seg and runs of their own lengths.
All inputs are finite; a program needn't handle non-finite values.
Results may differ from a plain program's by a relative error of at most 0.023.
Values may be sent and summed in bfloat16 or wider, within the bound.
No kernel may reach another device: no remote copies, remote signals or barrier semaphores. Data moves between devices by JAX's collectives and lax.ppermute only.
A program may use at most 256 MiB of HBM per device.

v0:
```python
import jax
import jax.numpy as jnp
from jax import lax
from jax.sharding import PartitionSpec as P

HEADS = 12
HEAD_DIM = 64
SEQ_MAX = 512


EPSILON = 1e-05
NEG_FILL = -1e30


def layer_norm(resid, gain, shift):
    center = resid - jnp.mean(resid, axis=-1, keepdims=True)
    spread = jnp.mean(center * center, axis=-1, keepdims=True)
    return center * lax.rsqrt(spread + EPSILON) * gain + shift


def norm_back(resid, gain, shift, upstream):
    _, pull = jax.vjp(layer_norm, resid, gain, shift)
    return pull(upstream)


def gelu_exact(value):
    return jax.nn.gelu(value, approximate=False)


def project(left, right):
    return jnp.dot(left, right, preferred_element_type=jnp.float32)


def back_project(grad, weight):
    return lax.dot_general(
        grad, weight, (((1,), (1,)), ((), ())), preferred_element_type=jnp.float32
    )


def weight_grad(acts, grad):
    return lax.dot_general(acts, grad, (((0,), (0,)), ((), ())), preferred_element_type=jnp.float32)


def column_sum(grad):
    return jnp.sum(grad.astype(jnp.float32), axis=0)


def split_heads(rows):
    return rows.reshape(rows.shape[0] // SEQ_MAX, SEQ_MAX, HEADS, HEAD_DIM)


def block_scores(queries, keys, query_ids, key_ids):
    scores = jnp.einsum(
        "qhd,khd->hqk", queries, keys, preferred_element_type=jnp.float32
    ) * HEAD_DIM ** (-0.5)
    same = query_ids[None, :, None] == key_ids[None, None, :]
    return jnp.where(same, scores, NEG_FILL)


def attend_block(items):
    queries, keys, values, query_ids, key_ids = items
    scores = block_scores(queries, keys, query_ids, key_ids)
    peak = jnp.max(scores, axis=-1, keepdims=True)
    weights = jnp.exp(scores - peak)
    total = jnp.sum(weights, axis=-1, keepdims=True)
    attention = (weights / total).astype(jnp.bfloat16)
    result = jnp.einsum("hqk,khd->qhd", attention, values, preferred_element_type=jnp.float32)
    return (result.astype(jnp.bfloat16), (peak + jnp.log(total))[..., 0])


def attend(queries, keys, values, query_ids, key_ids):
    items = (
        split_heads(queries),
        split_heads(keys),
        split_heads(values),
        query_ids.reshape(-1, SEQ_MAX),
        key_ids.reshape(-1, SEQ_MAX),
    )
    result, log_total = lax.map(attend_block, items)
    return (result.reshape(queries.shape), log_total)


def attend_back_block(items):
    queries, keys, values, query_ids, key_ids, log_total, upstream = items
    scores = block_scores(queries, keys, query_ids, key_ids)
    attention = jnp.exp(scores - log_total[..., None])
    value_grad = jnp.einsum(
        "hqk,qhd->khd", attention.astype(jnp.bfloat16), upstream, preferred_element_type=jnp.float32
    )
    attention_grad = jnp.einsum(
        "qhd,khd->hqk", upstream, values, preferred_element_type=jnp.float32
    )
    center = jnp.sum(attention * attention_grad, axis=-1, keepdims=True)
    score_grad = (attention * (attention_grad - center)).astype(jnp.bfloat16)
    scale = HEAD_DIM ** (-0.5)
    query_grad = (
        jnp.einsum("hqk,khd->qhd", score_grad, keys, preferred_element_type=jnp.float32) * scale
    )
    key_grad = (
        jnp.einsum("hqk,qhd->khd", score_grad, queries, preferred_element_type=jnp.float32) * scale
    )
    return (
        query_grad.astype(jnp.bfloat16),
        key_grad.astype(jnp.bfloat16),
        value_grad.astype(jnp.bfloat16),
    )


def attend_back(queries, keys, values, query_ids, key_ids, log_total, upstream):
    items = (
        split_heads(queries),
        split_heads(keys),
        split_heads(values),
        query_ids.reshape(-1, SEQ_MAX),
        key_ids.reshape(-1, SEQ_MAX),
        log_total,
        split_heads(upstream),
    )
    query_grad, key_grad, value_grad = lax.map(attend_back_block, items)
    return (
        query_grad.reshape(queries.shape),
        key_grad.reshape(keys.shape),
        value_grad.reshape(values.shape),
    )


def gather_forward(shards):
    projections, out_weights, biases, gains, shifts, in_weights, in_bias, out_ffn, out_bias = shards
    return (
        lax.all_gather(projections, ("dp", "fsdp"), axis=1, tiled=True),
        lax.all_gather(out_weights, ("dp", "fsdp"), axis=1, tiled=True),
        lax.all_gather(biases, ("dp", "fsdp"), axis=1, tiled=True),
        lax.all_gather(gains, ("dp", "fsdp"), axis=1, tiled=True),
        lax.all_gather(shifts, ("dp", "fsdp"), axis=1, tiled=True),
        lax.all_gather(in_weights, ("dp", "fsdp"), axis=0, tiled=True),
        lax.all_gather(in_bias, ("dp", "fsdp"), axis=0, tiled=True),
        lax.all_gather(out_ffn, ("dp", "fsdp"), axis=0, tiled=True),
        lax.all_gather(out_bias, ("dp", "fsdp"), axis=0, tiled=True),
    )


def gather_backward(shards):
    projections, out_weights, biases, gains, shifts, in_weights, in_bias, out_ffn, out_bias = shards
    return (
        lax.all_gather(projections, ("dp", "fsdp"), axis=1, tiled=True),
        lax.all_gather(out_weights, ("dp", "fsdp"), axis=1, tiled=True),
        lax.all_gather(biases, ("dp", "fsdp"), axis=1, tiled=True),
        lax.all_gather(gains, ("dp", "fsdp"), axis=1, tiled=True),
        lax.all_gather(shifts, ("dp", "fsdp"), axis=1, tiled=True),
        lax.all_gather(in_weights, ("dp", "fsdp"), axis=0, tiled=True),
        lax.all_gather(in_bias, ("dp", "fsdp"), axis=0, tiled=True),
        lax.all_gather(out_ffn, ("dp", "fsdp"), axis=0, tiled=True),
        lax.all_gather(out_bias, ("dp", "fsdp"), axis=0, tiled=True),
    )


def reduce_grads(grads):
    (
        proj_grad,
        outw_grad,
        bias_grad,
        gain_grad,
        shift_grad,
        inw_grad,
        inb_grad,
        outf_grad,
        outb_grad,
    ) = grads
    return (
        lax.psum_scatter(proj_grad, ("dp", "fsdp"), scatter_dimension=1, tiled=True),
        lax.psum_scatter(outw_grad, ("dp", "fsdp"), scatter_dimension=1, tiled=True),
        lax.psum_scatter(bias_grad, ("dp", "fsdp"), scatter_dimension=1, tiled=True),
        lax.psum_scatter(gain_grad, ("dp", "fsdp"), scatter_dimension=1, tiled=True),
        lax.psum_scatter(shift_grad, ("dp", "fsdp"), scatter_dimension=1, tiled=True),
        lax.psum_scatter(inw_grad, ("dp", "fsdp"), scatter_dimension=0, tiled=True),
        lax.psum_scatter(inb_grad, ("dp", "fsdp"), scatter_dimension=0, tiled=True),
        lax.psum_scatter(outf_grad, ("dp", "fsdp"), scatter_dimension=0, tiled=True),
        lax.psum_scatter(outb_grad, ("dp", "fsdp"), scatter_dimension=0, tiled=True),
    )


def forward_pass(query, memory, query_seg, memory_seg, params):
    projections, out_weights, biases, gains, shifts, in_weights, in_bias, out_ffn, out_bias = params
    biases = biases.astype(jnp.float32)
    gains = gains.astype(jnp.float32)
    shifts = shifts.astype(jnp.float32)
    self_queries = (project(query, projections[0]) + biases[0]).astype(jnp.bfloat16)
    self_keys = project(query, projections[1]).astype(jnp.bfloat16)
    self_values = (project(query, projections[2]) + biases[1]).astype(jnp.bfloat16)
    self_mixed, self_total = attend(self_queries, self_keys, self_values, query_seg, query_seg)
    first_sum = query.astype(jnp.float32) + project(self_mixed, out_weights[0]) + biases[2]
    first = layer_norm(first_sum, gains[0], shifts[0])
    first_low = first.astype(jnp.bfloat16)
    cross_queries = (project(first_low, projections[3]) + biases[3]).astype(jnp.bfloat16)
    cross_keys = project(memory, projections[4]).astype(jnp.bfloat16)
    cross_values = (project(memory, projections[5]) + biases[4]).astype(jnp.bfloat16)
    cross_mixed, cross_total = attend(
        cross_queries, cross_keys, cross_values, query_seg, memory_seg
    )
    second_sum = first + project(cross_mixed, out_weights[1]) + biases[5]
    second = layer_norm(second_sum, gains[1], shifts[1])
    second_low = second.astype(jnp.bfloat16)
    hidden_pre = project(second_low, in_weights) + in_bias.astype(jnp.float32)
    hidden = gelu_exact(hidden_pre).astype(jnp.bfloat16)
    third_sum = second + project(hidden, out_ffn) + out_bias.astype(jnp.float32)
    output = layer_norm(third_sum, gains[2], shifts[2])
    return (
        output,
        self_queries,
        self_keys,
        self_values,
        self_mixed,
        self_total,
        first_sum,
        first_low,
        cross_queries,
        cross_keys,
        cross_values,
        cross_mixed,
        cross_total,
        second_sum,
        second_low,
        hidden_pre,
        hidden,
        third_sum,
    )


def body(
    query,
    memory,
    query_seg,
    memory_seg,
    attn_proj,
    attn_out,
    attn_bias,
    norm_gain,
    norm_bias,
    ffn_in,
    ffn_in_bias,
    ffn_out,
    ffn_out_bias,
    cotangent,
):
    shards = (
        attn_proj,
        attn_out,
        attn_bias,
        norm_gain,
        norm_bias,
        ffn_in,
        ffn_in_bias,
        ffn_out,
        ffn_out_bias,
    )
    first_params = gather_forward(shards)
    mixed = forward_pass(query, memory, query_seg, memory_seg, first_params)[0].astype(jnp.bfloat16)
    params = gather_backward(shards)
    (
        _,
        self_queries,
        self_keys,
        self_values,
        self_mixed,
        self_total,
        first_sum,
        first_low,
        cross_queries,
        cross_keys,
        cross_values,
        cross_mixed,
        cross_total,
        second_sum,
        second_low,
        hidden_pre,
        hidden,
        third_sum,
    ) = forward_pass(query, memory, query_seg, memory_seg, params)
    projections, out_weights, biases, gains, shifts, in_weights, in_bias, out_ffn, out_bias = params
    gains = gains.astype(jnp.float32)
    shifts = shifts.astype(jnp.float32)
    third_grad, gain_last, shift_last = norm_back(
        third_sum, gains[2], shifts[2], cotangent.astype(jnp.float32)
    )
    branch_grad = third_grad.astype(jnp.bfloat16)
    out_ffn_grad = weight_grad(hidden, branch_grad)
    out_bias_grad = column_sum(branch_grad)
    hidden_grad = back_project(branch_grad, out_ffn)
    _, gelu_pull = jax.vjp(gelu_exact, hidden_pre)
    pre_grad = gelu_pull(hidden_grad)[0].astype(jnp.bfloat16)
    in_weights_grad = weight_grad(second_low, pre_grad)
    in_bias_grad = column_sum(pre_grad)
    second_grad = third_grad + back_project(pre_grad, in_weights)
    second_sum_grad, gain_mid, shift_mid = norm_back(second_sum, gains[1], shifts[1], second_grad)
    cross_branch = second_sum_grad.astype(jnp.bfloat16)
    cross_out_grad = weight_grad(cross_mixed, cross_branch)
    cross_out_bias = column_sum(cross_branch)
    cross_mixed_grad = back_project(cross_branch, out_weights[1]).astype(jnp.bfloat16)
    cross_query_grad, cross_key_grad, cross_value_grad = attend_back(
        cross_queries,
        cross_keys,
        cross_values,
        query_seg,
        memory_seg,
        cross_total,
        cross_mixed_grad,
    )
    cross_query_proj = weight_grad(first_low, cross_query_grad)
    cross_key_proj = weight_grad(memory, cross_key_grad)
    cross_value_proj = weight_grad(memory, cross_value_grad)
    memory_grad = back_project(cross_key_grad, projections[4]) + back_project(
        cross_value_grad, projections[5]
    )
    first_grad = second_sum_grad + back_project(cross_query_grad, projections[3])
    first_sum_grad, gain_top, shift_top = norm_back(first_sum, gains[0], shifts[0], first_grad)
    self_branch = first_sum_grad.astype(jnp.bfloat16)
    self_out_grad = weight_grad(self_mixed, self_branch)
    self_out_bias = column_sum(self_branch)
    self_mixed_grad = back_project(self_branch, out_weights[0]).astype(jnp.bfloat16)
    self_query_grad, self_key_grad, self_value_grad = attend_back(
        self_queries, self_keys, self_values, query_seg, query_seg, self_total, self_mixed_grad
    )
    query_grad = (
        first_sum_grad
        + back_project(self_query_grad, projections[0])
        + back_project(self_key_grad, projections[1])
        + back_project(self_value_grad, projections[2])
    )
    proj_grads = jnp.stack(
        [
            weight_grad(query, self_query_grad),
            weight_grad(query, self_key_grad),
            weight_grad(query, self_value_grad),
            cross_query_proj,
            cross_key_proj,
            cross_value_proj,
        ]
    )
    out_grads = jnp.stack([self_out_grad, cross_out_grad])
    bias_grads = jnp.stack(
        [
            column_sum(self_query_grad),
            column_sum(self_value_grad),
            self_out_bias,
            column_sum(cross_query_grad),
            column_sum(cross_value_grad),
            cross_out_bias,
        ]
    )
    gain_grads = jnp.stack([gain_top, gain_mid, gain_last])
    shift_grads = jnp.stack([shift_top, shift_mid, shift_last])
    owned = reduce_grads(
        (
            proj_grads,
            out_grads,
            bias_grads,
            gain_grads,
            shift_grads,
            in_weights_grad,
            in_bias_grad,
            out_ffn_grad,
            out_bias_grad,
        )
    )
    return (
        mixed,
        query_grad,
        memory_grad,
        owned[0],
        owned[1],
        owned[2],
        owned[3],
        owned[4],
        owned[5],
        owned[6],
        owned[7],
        owned[8],
    )


def solution(mesh):
    placed = (
        P(("dp", "fsdp"), None),
        P(("dp", "fsdp"), None),
        P(("dp", "fsdp")),
        P(("dp", "fsdp")),
        P(None, ("dp", "fsdp"), None),
        P(None, ("dp", "fsdp"), None),
        P(None, ("dp", "fsdp")),
        P(None, ("dp", "fsdp")),
        P(None, ("dp", "fsdp")),
        P(("dp", "fsdp"), None),
        P(("dp", "fsdp")),
        P(("dp", "fsdp"), None),
        P(("dp", "fsdp")),
        P(("dp", "fsdp"), None),
    )
    return jax.shard_map(
        body,
        mesh=mesh,
        in_specs=placed,
        out_specs=(
            P(("dp", "fsdp"), None),
            P(("dp", "fsdp"), None),
            P(("dp", "fsdp"), None),
            P(None, ("dp", "fsdp"), None),
            P(None, ("dp", "fsdp"), None),
            P(None, ("dp", "fsdp")),
            P(None, ("dp", "fsdp")),
            P(None, ("dp", "fsdp")),
            P(("dp", "fsdp"), None),
            P(("dp", "fsdp")),
            P(("dp", "fsdp"), None),
            P(("dp", "fsdp")),
        ),
        check_vma=False,
    )
```

profile of v0, /device:TPU:0, one launch (start us, length us, event | category | flops | bytes accessed | tf_op | source)
XLA Modules:
  0.0 1427.2 jit_solution(13525923805653021669)
XLA Ops:
  10.1 71.0 %all-gather = bf16[32,24,6]{1,2,0:T(8,128)(2,1)S(1)} all-gather(bf16[1,24,6]{1,2,0:T(8,128)(2,1)} %bitcast.567), channel_id=1, replica_groups=mesh['dp'=4,'fsdp'=8] {'dp','fsdp'}, dimensions={0}, use_global_device_ids=true | all-gather | bytes 9504 | tf_op jit(solution)/shard_map/all_gather | solution.py:132
  85.4 63.4 %all-gather.1 = bf16[32,24,3]{1,2,0:T(4,128)(2,1)S(1)} all-gather(bf16[1,24,3]{1,2,0:T(4,128)(2,1)S(1)} %bitcast.568), channel_id=1, replica_groups=mesh['dp'=4,'fsdp'=8] {'dp','fsdp'}, dimensions={0}, use_global_device_ids=true | all-gather | bytes 4752 | tf_op jit(solution)/shard_map/all_gather | solution.py:133
  149.1 65.8 %all-gather.2 = bf16[32,24,3]{1,2,0:T(4,128)(2,1)S(1)} all-gather(bf16[1,24,3]{1,2,0:T(4,128)(2,1)S(1)} %bitcast.569), channel_id=1, replica_groups=mesh['dp'=4,'fsdp'=8] {'dp','fsdp'}, dimensions={0}, use_global_device_ids=true | all-gather | bytes 4752 | tf_op jit(solution)/shard_map/all_gather | solution.py:134
  215.7 37.3 %all-reduce.8 = (bf16[3072]{0:T(1024)(128)(2,1)S(1)}, bf16[768]{0:T(1024)(128)(2,1)S(1)}) all-reduce(bf16[3072]{0:T(1024)(128)(2,1)S(1)} %dynamic-update-slice, bf16[768]{0:T(1024)(128)(2,1)S(1)} %dynamic-update-slice.1), channel_id=1, replica_groups=mesh['dp'=4,'fsdp'=8] {'dp','fsdp'}, use_global_device_ids=true, to_apply=%add | all-reduce | flops 3840 | bytes 15360
  292.2 35.0 %while.75 = (s32[]{:T(128)}, bf16[2,512,12,64]{1,3,2,0:T(8,128)(2,1)}, bf16[2,512,12,64]{1,3,2,0:T(8,128)(2,1)}, s32[2,512]{1,0:T(2,128)S(1)}, bf16[2,512,12,64]...) while((s32[]{:T(128)}, bf16[2,512,12,64]{1,3,2,0:T(8,128)(2,1)}, ...), condition=%wide.region_3.4_spmd, body=%wide.region_0.3_spmd.sunk | while | flops 824836608 | bytes 28893264 | solution.py:79
  292.6 10.3 fusion.413
  310.0 10.3 fusion.413
  371.3 34.9 %while.76 = (s32[]{:T(128)}, bf16[2,512,12,64]{1,3,2,0:T(8,128)(2,1)}, bf16[2,512,12,64]{1,3,2,0:T(8,128)(2,1)}, s32[2,512]{1,0:T(2,128)S(1)}, s32[2,512]{1,0:T(...) while((s32[]{:T(128)}, ...), condition=%wide.region_9.10_spmd, body=%wide.region_6.9_spmd.sunk | while | flops 824836608 | bytes 28899416 | solution.py:79
  414.4 37.1 %fusion.221.clone.4 = bf16[1024,3072]{1,0:T(8,128)(2,1)} fusion(f32[3072]{0:T(1024)S(1)} %copy-done.109, bf16[768,3072]{1,0:T(8,128)(2,1)} %all-gather.12.cloned.1.call-done, f32[1024,768]{0,1:T(8,128)} %copy-done.47, f32[768]{0:T(1024)S(1)} %copy-done.118, f32[768]{0:T(1024)S(1)} %copy-done.101, ...), kind=kOutput, calls=%fused_computation.197.clone.clone.clone.clone.clone.clone.1 | convolution fusion | flops 5043388416 | bytes 14182400 | tf_op jit(solution)/shard_map/dot_general | solution.py:31
  465.0 23.0 %while.77 = (s32[]{:T(128)}, bf16[2,512,12,64]{1,3,2,0:T(8,128)(2,1)}, f32[2,12,512]{2,1,0:T(8,128)S(1)}, bf16[2,512,12,64]{1,3,2,0:T(8,128)(2,1)}, s32[2,512]{1...) while((s32[]{:T(128)}, ...), condition=%wide.region_17.18_spmd, body=%wide.region_14.17_spmd.sunk | while | flops 843704320 | bytes 42172508 | solution.py:79
  506.5 23.3 %while.78 = (s32[]{:T(128)}, bf16[2,512,12,64]{1,3,2,0:T(8,128)(2,1)}, f32[2,12,512]{2,1,0:T(8,128)S(1)}, bf16[2,512,12,64]{1,3,2,0:T(8,128)(2,1)}, s32[2,512]{1...) while((s32[]{:T(128)}, ...), condition=%wide.region_23.24_spmd, body=%wide.region_20.23_spmd.sunk | while | flops 843704320 | bytes 42178660 | solution.py:79
  538.7 37.5 %multiply_convert_fusion.6 = (bf16[1024,3072]{1,0:T(8,128)(2,1)S(1)}, f32[1024,3072]{1,0:T(8,128)}, f32[1024,3072]{1,0:T(8,128)}) fusion(f32[3072]{0:T(1024)S(1)} %copy-done.110, bf16[768,3072]{1,0:T(8,128)(2,1)S(1)} %bitcast.571, f32[1024,768]{0,1:T(8,128)S(1)} %get-tuple-element.759, f32[1024]{0:T(1024)S(1)} %fusion.237, ...), kind=kOutput, calls=%fused_computation.201 | convolution fusion | flops 5043388416 | bytes 39348224 | tf_op jit(solution)/shard_map/dot_general | solution.py:31
  589.9 19.2 %convert_reduce_fusion = (f32[3072]{0:T(1024)}, bf16[1024,3072]{1,0:T(8,128)(2,1)}) fusion(f32[1024,3072]{1,0:T(8,128)} %get-tuple-element.734, bf16[1024,768]{0,1:T(8,128)(2,1)} %get-tuple-element.724, bf16[3072,768]{1,0:T(8,128)(2,1)} %all-gather.14.cloned.1.call-done, f32[1024,3072]{1,0:T(8,128)} %get-tuple-element.760, f32[3072]{0:T(1024)S(1)} %copy-done.110), kind=kOutput, calls=%fused_computation.199 | convolution fusion | flops 4885312512 | bytes 37773312 | tf_op jit(solution)/shard_map/dot_general | solution.py:35
  609.1 11.4 multiply_reduce_fusion.2
  638.8 52.2 %while.79 = (s32[]{:T(128)}, bf16[2,512,12,64]{1,3,2,0:T(8,128)(2,1)}, bf16[2,512,12,64]{1,3,2,0:T(8,128)(2,1)}, bf16[2,512,12,64]{1,3,2,0:T(8,128)(2,1)}, bf16[...) while((s32[]{:T(128)}, ...), condition=%wide.region_34.35_spmd, body=%wide.region_32.34_spmd.sunk | while | flops 2062673920 | bytes 153822576 | solution.py:119
  717.8 52.1 %while.80 = (s32[]{:T(128)}, bf16[2,512,12,64]{1,3,2,0:T(8,128)(2,1)}, bf16[2,512,12,64]{1,3,2,0:T(8,128)(2,1)}, bf16[2,512,12,64]{1,3,2,0:T(8,128)(2,1)}, bf16[...) while((s32[]{:T(128)}, ...), condition=%wide.region_39.40_spmd, body=%wide.region_37.39_spmd.sunk | while | flops 2062673920 | bytes 153816432 | solution.py:119
  799.2 17.5 %copy.261 = f32[6,768,768]{2,0,1:T(8,128)} copy(f32[6,768,768]{1,2,0:T(8,128)} %bitcast_dynamic-update-slice_fusion.2) | data formatting | bytes 28311552 | tf_op jit(solution)/shard_map/stack | solution.py:329
  824.9 11.1 fusion.269
  837.6 10.9 fusion.303
  871.3 44.9 %all-reduce.7 = (f32[6,768]{1,0:T(8,128)S(1)}, f32[3,768]{1,0:T(4,128)S(1)}, f32[3,768]{1,0:T(4,128)S(1)}, f32[3072]{0:T(1024)S(1)}, f32[768]{0:T(1024)S(1)}) all-reduce(f32[6,768]{1,0:T(8,128)S(1)} %stack.79, f32[3,768]{1,0:T(4,128)S(1)} %pad_maximum_fusion.1, ...), channel_id=4, replica_groups=mesh['dp'=4,'fsdp'=8] {'dp','fsdp'}, use_global_device_ids=true, to_apply=%region_48.49.clone | all-reduce | flops 13056 | bytes 104448
  927.1 98.0 %reduce-scatter.8.cloned.1.call-done = f32[6,24,768]{2,0,1:T(8,128)} async-done(((f32[6,768,768]{2,0,1:T(8,128)}), f32[6,24,768]{2,0,1:T(8,128)}) %reduce-scatter.8.cloned.1.call-update) | async-done | bytes 442384 | tf_op jit(solution)/shard_map/reduce_scatter | solution.py:170
  1027.0 109.9 %reduce-scatter.10.cloned.1.call-done = f32[2,24,768]{2,1,0:T(8,128)} async-done(((f32[2,768,768]{2,1,0:T(8,128)}), f32[2,24,768]{2,1,0:T(8,128)}) %reduce-scatter.10.cloned.1.call-update) | async-done | bytes 147472 | tf_op jit(solution)/shard_map/reduce_scatter | solution.py:171
  1136.9 142.2 %reduce-scatter.12.cloned.1.call-done = f32[24,3072]{1,0:T(8,128)} async-done(((f32[768,3072]{1,0:T(8,128)}), f32[24,3072]{1,0:T(8,128)}) %reduce-scatter.12.cloned.1.call-update) | async-done | bytes 294928 | tf_op jit(solution)/shard_map/reduce_scatter | solution.py:175
  1279.2 141.0 %reduce-scatter.14.cloned.1.call-done = f32[96,768]{1,0:T(8,128)} async-done(((f32[3072,768]{1,0:T(8,128)}), f32[96,768]{1,0:T(8,128)}) %reduce-scatter.14.cloned.1.call-update) | async-done | bytes 294928 | tf_op jit(solution)/shard_map/reduce_scatter | solution.py:177
  (582 shorter events, 470.3 us)
Async XLA Ops:
  7.2 342.4 %copy-start = (bf16[1024,768]{1,0:T(8,128)(2,1)S(1)}, bf16[1024,768]{1,0:T(8,128)(2,1)}, u32[]{:S(2)}) copy-start(bf16[1024,768]{1,0:T(8,128)(2,1)} %param.27) | copy-start | bytes 4718596
  7.2 78.2 %copy-start.130 = (bf16[3,24]{1,0:T(4,128)(2,1)S(1)}, bf16[3,24]{1,0:T(4,128)(2,1)}, u32[]{:S(2)}) copy-start(bf16[3,24]{1,0:T(4,128)(2,1)} %param.33) | copy-start | bytes 436
  7.2 141.9 %copy-start.131 = (bf16[3,24]{1,0:T(4,128)(2,1)S(1)}, bf16[3,24]{1,0:T(4,128)(2,1)}, u32[]{:S(2)}) copy-start(bf16[3,24]{1,0:T(4,128)(2,1)} %param.34) | copy-start | bytes 436
  7.2 208.0 %copy-start.117 = (s32[1024]{0:T(1024)S(1)}, s32[1024]{0:T(1024)}, u32[]{:S(2)}) copy-start(s32[1024]{0:T(1024)} %param.29) | copy-start | bytes 12292
  7.2 208.0 %copy-start.137 = (bf16[96]{0:T(256)(128)(2,1)S(1)}, bf16[96]{0:T(256)(128)(2,1)}, u32[]{:S(2)}) copy-start(bf16[96]{0:T(256)(128)(2,1)} %param.36) | copy-start | bytes 580
  7.2 208.3 %copy-start.138 = (bf16[24]{0:T(256)(128)(2,1)S(1)}, bf16[24]{0:T(256)(128)(2,1)}, u32[]{:S(2)}) copy-start(bf16[24]{0:T(256)(128)(2,1)} %param.38) | copy-start | bytes 148
  7.2 247.0 %copy-start.49 = (bf16[1024,768]{1,0:T(8,128)(2,1)S(1)}, bf16[1024,768]{1,0:T(8,128)(2,1)}, u32[]{:S(2)}) copy-start(bf16[1024,768]{1,0:T(8,128)(2,1)} %param.39) | copy-start | bytes 4718596
  7.3 249.2 %all-gather.8.cloned.1.call-start = ((), (), s32[]{:S(2)}) async-start(), calls=%async_computation.4 | async-start | bytes 7299072 | tf_op jit(solution)/shard_map/all_gather | solution.py:130
  8.0 324.4 %all-gather.10.cloned.1.call-start = ((), (), s32[]{:S(2)}) async-start(), calls=%async_computation.5 | async-start | bytes 2433024 | tf_op jit(solution)/shard_map/all_gather | solution.py:131
  8.7 405.7 %all-gather.12.cloned.1.call-start = ((), (), s32[]{:S(2)}) async-start(), calls=%async_computation.6 | async-start | bytes 4866048 | tf_op jit(solution)/shard_map/all_gather | solution.py:135
  9.5 442.1 %all-gather.14.cloned.1.call-start = ((), (), s32[]{:S(2)}) async-start(), calls=%async_computation.7 | async-start | bytes 4866048 | tf_op jit(solution)/shard_map/all_gather | solution.py:137
  10.1 1015.0 %reduce-scatter.8.cloned.1.call-start = ((), (), s32[]{:S(2)}) async-start(), calls=%async_computation.8 | async-start | bytes 19464192 | tf_op jit(solution)/shard_map/reduce_scatter | solution.py:170
  82.0 250.4 %copy-start.128 = (f32[768]{0:T(1024)}, f32[768]{0:T(1024)S(1)}, u32[]{:S(2)}) copy-start(f32[768]{0:T(1024)S(1)} %get-tuple-element.609) | copy-start | bytes 9220
  82.0 254.7 %copy-start.126 = (f32[768]{0:T(1024)}, f32[768]{0:T(1024)S(1)}, u32[]{:S(2)}) copy-start(f32[768]{0:T(1024)S(1)} %get-tuple-element.607) | copy-start | bytes 9220
  256.5 153.8 %copy-start.104 = (f32[768]{0:T(1024)}, f32[768]{0:T(1024)S(1)}, u32[]{:S(2)}) copy-start(f32[768]{0:T(1024)S(1)} %get-tuple-element.773) | copy-start | bytes 9220
  256.5 153.8 %copy-start.121 = (f32[768]{0:T(1024)}, f32[768]{0:T(1024)S(1)}, u32[]{:S(2)}) copy-start(f32[768]{0:T(1024)S(1)} %get-tuple-element.617) | copy-start | bytes 9220
  493.4 40.6 %copy-start.80 = (f32[1024]{0:T(1024)}, f32[1024]{0:T(1024)S(1)}, u32[]{:S(2)}) copy-start(f32[1024]{0:T(1024)S(1)} %broadcast_multiply_fusion.2) | copy-start | bytes 12292
  534.0 42.1 %slice-start.2 = ((s8[4718592]{0:T(1024)(128)(4,1)}), s8[4194304]{0:T(1024)(128)(4,1)S(1)}, s32[]{:S(2)}) async-start(s8[4718592]{0:T(1024)(128)(4,1)} %bitcast.572), calls=%async_computation.14 | async-start | bytes 8388608
  536.1 40.1 %copy-start.30 = (f32[1024,768]{0,1:T(8,128)}, f32[1024,768]{0,1:T(8,128)S(1)}, u32[]{:S(2)}) copy-start(f32[1024,768]{0,1:T(8,128)S(1)} %get-tuple-element.759) | copy-start | bytes 9437188
  536.1 84.4 %copy-start.83 = (f32[1024]{0:T(1024)}, f32[1024]{0:T(1024)S(1)}, u32[]{:S(2)}) copy-start(f32[1024]{0:T(1024)S(1)} %broadcast_multiply_fusion.1) | copy-start | bytes 12292
  538.7 81.8 %copy-start.98 = (f32[1024]{0:T(1024)}, f32[1024]{0:T(1024)S(1)}, u32[]{:S(2)}) copy-start(f32[1024]{0:T(1024)S(1)} %fusion.237) | copy-start | bytes 12292
  816.8 320.2 %reduce-scatter.10.cloned.1.call-start = ((), (), s32[]{:S(2)}) async-start(), calls=%async_computation.9 | async-start | bytes 4866048 | tf_op jit(solution)/shard_map/reduce_scatter | solution.py:171
  824.2 455.0 %reduce-scatter.12.cloned.1.call-start = ((), (), s32[]{:S(2)}) async-start(), calls=%async_computation.10 | async-start | bytes 9732096 | tf_op jit(solution)/shard_map/reduce_scatter | solution.py:175
  836.0 584.1 %reduce-scatter.14.cloned.1.call-start = ((), (), s32[]{:S(2)}) async-start(), calls=%async_computation.11 | async-start | bytes 9732096 | tf_op jit(solution)/shard_map/reduce_scatter | solution.py:177
  (144 other events, 566.3 us)
Sparse Core Ops, SparseCore 0:
  11.0 75.5 all-gather.7
  89.4 56.0 all-gather.9
  148.4 62.4 all-gather.11
  213.7 62.5 all-gather.13
  816.9 208.1 reduce-scatter.7
  1031.0 105.9 reduce-scatter.9
  1144.4 134.7 reduce-scatter.11
  1285.7 134.4 reduce-scatter.13
where the time goes:
time: 1440 us; the launch traced here: 1430 us
  waiting for transfers between devices  494 us (34%)
  matrix products  403 us (28%)
  blocking collectives  282 us (20%)
  local copies, waits for them, and re-layouts  167 us (12%)
  other arithmetic  62.9 us (4%)
  between operations  16.1 us (1%)
    reduce_scatter x1, waiting for transfers between devices, reduce_grads(): lax.psum_scatter(inw_grad, ('dp', 'fsdp'), scatter_dimension=0, tiled=True)  142 us
    reduce_scatter x1, waiting for transfers between devices, reduce_grads(): lax.psum_scatter(outf_grad, ('dp', 'fsdp'), scatter_dimension=0, tiled=True)  141 us
    dot_general x15, matrix products, project(): return jnp.dot(left, right, preferred_element_type=jnp.float32)  128 us
    reduce_scatter x1, waiting for transfers between devices, reduce_grads(): lax.psum_scatter(outw_grad, ('dp', 'fsdp'), scatter_dimension=1, tiled=True)  110 us
    reduce_scatter x1, waiting for transfers between devices, reduce_grads(): lax.psum_scatter(proj_grad, ('dp', 'fsdp'), scatter_dimension=1, tiled=True)  98 us
    unnamed x2, blocking collectives  82.2 us
    all_gather x1, blocking collectives, gather_forward(): lax.all_gather(biases, ('dp', 'fsdp'), axis=1, tiled=True)  71 us
    all_gather x1, blocking collectives, gather_forward(): lax.all_gather(shifts, ('dp', 'fsdp'), axis=1, tiled=True)  65.8 us
  transfers between devices with their start and end apart: 8, of which 4 were waited for; matrix products, arithmetic and copies ran while one was open for 18% of the time, Pallas kernels for 0%

commit v1 on v0

v1 whole, which is shorter than its diff:
```python
import functools

import jax
import jax.numpy as jnp
from jax import lax
from jax.experimental import pallas as pl
from jax.experimental.pallas import tpu as pltpu
from jax.sharding import PartitionSpec as P

HEADS = 12
HEAD_DIM = 64
SEQ_MAX = 512
PAIRS = HEADS // 2
EPSILON = 1e-05
MASKED = 1e30
SCALE = HEAD_DIM ** (-0.5)
BF = jnp.bfloat16
F32 = jnp.float32
VMEM_LIMIT = 60 * 1024 * 1024


def dot(left, right):
    return jnp.dot(left, right, preferred_element_type=F32)


def dot_nt(left, right):
    return lax.dot_general(left, right, (((1,), (1,)), ((), ())), preferred_element_type=F32)


def norm_parts(resid):
    center = resid - jnp.mean(resid, axis=-1, keepdims=True)
    rstd = lax.rsqrt(jnp.mean(center * center, axis=-1, keepdims=True) + EPSILON)
    return center * rstd, rstd


def norm_back(unit, rstd, gain, upstream):
    scaled = upstream * gain
    mean_s = jnp.mean(scaled, axis=-1, keepdims=True)
    mean_su = jnp.mean(scaled * unit, axis=-1, keepdims=True)
    grad = rstd * (scaled - mean_s - unit * mean_su)
    return grad, col_sum(upstream * unit), col_sum(upstream)


def col_sum(rows):
    return jnp.sum(rows, axis=0, keepdims=True)


def place_rows(rows, count):
    parts = list(rows)
    parts.append(jnp.zeros((count - len(parts), parts[0].shape[1]), F32))
    return jnp.concatenate(parts, axis=0)


def gelu_parts(value):
    size = jnp.abs(value) * (0.5**0.5)
    bell = jnp.exp(-0.5 * value * value)
    t = 1.0 / (1.0 + 0.3275911 * size)
    poly = t * (0.254829592 + t * (-0.284496736 + t * (1.421413741 + t * (-1.453152027 + t * 1.061405429))))
    tail = 0.5 * poly * bell
    phi = jnp.where(value >= 0, 1.0 - tail, tail)
    return value * phi, phi + value * (bell * (1.0 / (2.0 * 3.141592653589793) ** 0.5))


def left_half(shape):
    return lax.broadcasted_iota(jnp.int32, shape, 1) < HEAD_DIM


def head_pair(side, pair):
    return pl.ds(pl.multiple_of(pair * 128 + side * HEAD_DIM, HEAD_DIM), HEAD_DIM)


def key_tile(tile, marks, side):
    left = left_half(tile.shape)
    return jnp.where(left, tile, marks) if side == 0 else jnp.where(left, marks, tile)


def query_tile(rows, marks, side):
    return jnp.concatenate([rows, marks] if side == 0 else [marks, rows], axis=0)


def attend_block(k_ref, qt_ref, vt_ref, kmark_ref, qmark_ref, ot_ref, lse_ref):
    kmark = kmark_ref[...]
    qmark = qmark_ref[0]
    ones = jnp.ones((16, SEQ_MAX), BF)

    def one_pair(pair, carry):
        tile = k_ref[:, pl.ds(pl.multiple_of(pair * 128, 128), 128)]
        for side in range(2):
            rows = head_pair(side, pair)
            scores = dot(key_tile(tile, kmark, side), query_tile(qt_ref[rows, :], qmark, side))
            peak = jnp.max(scores, axis=0, keepdims=True)
            weights = jnp.exp(scores - peak).astype(BF)
            result = dot(jnp.concatenate([vt_ref[rows, :], ones], axis=0), weights)
            total = result[HEAD_DIM : HEAD_DIM + 1]
            ot_ref[rows, :] = (result[:HEAD_DIM] * (1.0 / total)).astype(BF)
            lse_ref[0, pl.ds(pair * 2 + side, 1), :] = peak + jnp.log(total)
        return carry

    lax.fori_loop(0, PAIRS, one_pair, 0)


def attend_back_block(
    q_ref, k_ref, v_ref, qt_ref, kt_ref, ot_ref, do_ref, dot_ref, kmark_ref, qmark_ref, lse_ref, dqt_ref, dk_ref, dv_ref
):
    kmark = kmark_ref[...]
    qmark = qmark_ref[0]
    left = left_half((SEQ_MAX, 128))
    blank = jnp.zeros((HEAD_DIM, SEQ_MAX), BF)

    def one_pair(pair, carry):
        cols = pl.ds(pl.multiple_of(pair * 128, 128), 128)
        k_tile, v_tile, q_tile, do_tile = k_ref[:, cols], v_ref[:, cols], q_ref[:, cols], do_ref[:, cols]
        value_grads, key_grads = [], []
        for side in range(2):
            rows = head_pair(side, pair)
            scores = dot(key_tile(k_tile, kmark, side), query_tile(qt_ref[rows, :], qmark, side))
            probs = jnp.exp(scores - lse_ref[0, pl.ds(pair * 2 + side, 1), :])
            value_grads.append(dot(probs.astype(BF), do_tile))
            up = dot_ref[rows, :]
            center = col_sum(up.astype(F32) * ot_ref[rows, :].astype(F32))
            probs_grad = dot(v_tile, query_tile(up, blank, side))
            score_grad = (probs * (probs_grad - center)).astype(BF)
            key_grads.append(dot(score_grad, q_tile))
            dqt_ref[rows, :] = (dot(kt_ref[rows, :], score_grad) * SCALE).astype(BF)
        dv_ref[:, cols] = jnp.where(left, value_grads[0], value_grads[1]).astype(BF)
        dk_ref[:, cols] = jnp.where(left, key_grads[0], key_grads[1]).astype(BF)
        return carry

    lax.fori_loop(0, PAIRS, one_pair, 0)


def self_forward_kernel(
    x_ref, w_ref, bias_ref, kmark_ref, qmark_ref, q_ref, k_ref, v_ref, ot_ref, lse_ref, qt_s, vt_s
):
    x = x_ref[...]
    queries = ((dot(x, w_ref[0]) + bias_ref[0:1]).astype(BF)) * SCALE
    q_ref[...] = queries
    qt_s[...] = queries.T
    k_ref[...] = dot(x, w_ref[1]).astype(BF)
    values = (dot(x, w_ref[2]) + bias_ref[1:2]).astype(BF)
    v_ref[...] = values
    vt_s[...] = values.T
    attend_block(k_ref, qt_s, vt_s, kmark_ref, qmark_ref, ot_ref, lse_ref)


def cross_forward_kernel(
    x_ref, mem_ref, sot_ref, wo_ref, w_ref, bias_ref, gain_ref, shift_ref, kmark_ref, qmark_ref,
    first_sum_ref, low_ref, q_ref, k_ref, v_ref, ot_ref, lse_ref, second_sum_ref, qt_s, vt_s,
):
    mem = mem_ref[...]
    k_ref[...] = dot(mem, w_ref[1]).astype(BF)
    values = (dot(mem, w_ref[2]) + bias_ref[4:5]).astype(BF)
    v_ref[...] = values
    vt_s[...] = values.T
    first_sum = x_ref[...].astype(F32) + (dot(sot_ref[...].T, wo_ref[0]) + bias_ref[2:3])
    first_sum_ref[...] = first_sum
    unit, _ = norm_parts(first_sum)
    first = unit * gain_ref[0:1] + shift_ref[0:1]
    low = first.astype(BF)
    low_ref[...] = low
    queries = ((dot(low, w_ref[0]) + bias_ref[3:4]).astype(BF)) * SCALE
    q_ref[...] = queries
    qt_s[...] = queries.T
    attend_block(k_ref, qt_s, vt_s, kmark_ref, qmark_ref, ot_ref, lse_ref)
    second_sum_ref[...] = first + (dot(ot_ref[...].T, wo_ref[1]) + bias_ref[5:6])


def feed_kernel(
    ss_ref, cot_ref, win_ref, bin_ref, wout_ref, bout_ref, gain_ref, shift_ref,
    mixed_ref, ssg_ref, dwin_ref, dwout_ref, dbin_ref, small_ref,
    low_s, lowt_s, hid_s, slope_s, acc_s, third_s, z_s,
):
    phase, chunk = pl.program_id(0), pl.program_id(1)
    last = pl.num_programs(1) - 1

    @pl.when((phase == 0) & (chunk == 0))
    def _():
        unit, _ = norm_parts(ss_ref[...])
        second = unit * gain_ref[1:2] + shift_ref[1:2]
        low = second.astype(BF)
        low_s[...] = low
        lowt_s[...] = low.T
        acc_s[...] = second + bout_ref[...]

    @pl.when(phase == 0)
    def _():
        pre = dot(low_s[...], win_ref[...]) + bin_ref[...]
        hidden, slope = gelu_parts(pre)
        hidden = hidden.astype(BF)
        hid_s[chunk] = hidden
        slope_s[chunk] = slope
        acc_s[...] += dot(hidden, wout_ref[...])

    @pl.when((phase == 1) & (chunk == 0))
    def _():
        unit, rstd = norm_parts(acc_s[...])
        mixed_ref[...] = (unit * gain_ref[2:3] + shift_ref[2:3]).astype(BF)
        third, dgain, dshift = norm_back(unit, rstd, gain_ref[2:3], cot_ref[...].astype(F32))
        z = third.astype(BF)
        z_s[...] = z
        acc_s[...] = third
        small_ref[...] = place_rows([dgain, dshift, col_sum(z.astype(F32))], 8)

    @pl.when(phase == 1)
    def _():
        z = z_s[...]
        pre_grad = (dot_nt(z, wout_ref[...]) * slope_s[chunk]).astype(BF)
        dbin_ref[...] = col_sum(pre_grad.astype(F32))
        dwout_ref[...] = dot(hid_s[chunk].T, z).astype(BF)
        dwin_ref[...] = dot(lowt_s[...], pre_grad).astype(BF)
        acc_s[...] += dot_nt(pre_grad, win_ref[...])

    @pl.when((phase == 1) & (chunk == last))
    def _():
        unit, rstd = norm_parts(ss_ref[...])
        grad, dgain, dshift = norm_back(unit, rstd, gain_ref[1:2], acc_s[...])
        ssg_ref[...] = grad
        small_ref[3:5] = jnp.concatenate([dgain, dshift], axis=0)


def add_to(ref, index, value, first):
    @pl.when(first)
    def _():
        ref[index] = value

    @pl.when(jnp.logical_not(first))
    def _():
        ref[index] += value


def cross_back_kernel(
    ssg_ref, fs_ref, low_ref, mem_ref, q_ref, k_ref, v_ref, ot_ref, lse_ref, wo_ref, w_ref, gain_ref, kmark_ref, qmark_ref,
    fsg_ref, mg_ref, dw_ref, small_ref,
    qt_s, kt_s, do_s, dot_s, dqt_s, dk_s, dv_s, acc_s, small_s,
):
    block = pl.program_id(0)
    first, last = block == 0, block == pl.num_programs(0) - 1
    upstream = ssg_ref[...]
    branch = upstream.astype(BF)
    out_grad = dot(ot_ref[...], branch)
    mixed_grad = dot_nt(branch, wo_ref[0]).astype(BF)
    do_s[...] = mixed_grad
    dot_s[...] = mixed_grad.T
    qt_s[...] = q_ref[...].T
    kt_s[...] = k_ref[...].T
    attend_back_block(
        q_ref, k_ref, v_ref, qt_s, kt_s, ot_ref, do_s, dot_s, kmark_ref, qmark_ref, lse_ref, dqt_s, dk_s, dv_s
    )
    dq = dqt_s[...].T
    dk, dv = dk_s[...], dv_s[...]
    mg_ref[...] = dot_nt(dk, w_ref[1]) + dot_nt(dv, w_ref[2])
    memt = mem_ref[...].T
    add_to(acc_s, 0, dot(low_ref[...].T, dq), first)
    add_to(acc_s, 1, dot(memt, dk), first)
    add_to(acc_s, 2, dot(memt, dv), first)
    add_to(acc_s, 3, out_grad, first)
    first_grad = upstream + dot_nt(dq, w_ref[0])
    unit, rstd = norm_parts(fs_ref[...])
    grad, dgain, dshift = norm_back(unit, rstd, gain_ref[0:1], first_grad)
    fsg_ref[...] = grad
    sums = [col_sum(dq.astype(F32)), col_sum(dv.astype(F32)), col_sum(branch.astype(F32)), dgain, dshift]
    add_to(small_s, slice(None), place_rows(sums, 8), first)

    @pl.when(last)
    def _():
        dw_ref[...] = acc_s[...].astype(BF)
        small_ref[...] = small_s[...]


def self_back_kernel(
    fsg_ref, x_ref, q_ref, k_ref, v_ref, ot_ref, lse_ref, wo_ref, w_ref, kmark_ref, qmark_ref,
    qg_ref, dw_ref, small_ref,
    qt_s, kt_s, do_s, dot_s, dqt_s, dk_s, dv_s, acc_s, small_s,
):
    block = pl.program_id(0)
    first, last = block == 0, block == pl.num_programs(0) - 1
    upstream = fsg_ref[...]
    branch = upstream.astype(BF)
    out_grad = dot(ot_ref[...], branch)
    mixed_grad = dot_nt(branch, wo_ref[0]).astype(BF)
    do_s[...] = mixed_grad
    dot_s[...] = mixed_grad.T
    qt_s[...] = q_ref[...].T
    kt_s[...] = k_ref[...].T
    attend_back_block(
        q_ref, k_ref, v_ref, qt_s, kt_s, ot_ref, do_s, dot_s, kmark_ref, qmark_ref, lse_ref, dqt_s, dk_s, dv_s
    )
    dq = dqt_s[...].T
    dk, dv = dk_s[...], dv_s[...]
    xt = x_ref[...].T
    add_to(acc_s, 0, dot(xt, dq), first)
    add_to(acc_s, 1, dot(xt, dk), first)
    add_to(acc_s, 2, dot(xt, dv), first)
    add_to(acc_s, 3, out_grad, first)
    qg_ref[...] = upstream + dot_nt(dq, w_ref[0]) + dot_nt(dk, w_ref[1]) + dot_nt(dv, w_ref[2])
    sums = [col_sum(dq.astype(F32)), col_sum(dv.astype(F32)), col_sum(branch.astype(F32))]
    add_to(small_s, slice(None), place_rows(sums, 8), first)

    @pl.when(last)
    def _():
        dw_ref[...] = acc_s[...].astype(BF)
        small_ref[...] = small_s[...]


def row_block(width):
    return pl.BlockSpec((SEQ_MAX, width), lambda b: (b, 0))


def col_block(height):
    return pl.BlockSpec((height, SEQ_MAX), lambda b: (0, b))


def lead_block(rows):
    return pl.BlockSpec((1, rows, SEQ_MAX), lambda b: (b, 0, 0))


def whole(array, **kw):
    zeros = (0,) * array.ndim
    return pl.BlockSpec(array.shape, lambda *_: zeros, pipeline_mode=pl.Buffered(1))


def params(semantics):
    return pltpu.CompilerParams(vmem_limit_bytes=VMEM_LIMIT, dimension_semantics=semantics)


def cost(flops, data, exps=0):
    return pl.CostEstimate(flops=int(flops), bytes_accessed=int(data), transcendentals=int(exps))


def shape(dims, kind):
    return jax.ShapeDtypeStruct(dims, kind)


def self_forward(x, w, bias, kmark, qmark):
    rows, d = x.shape
    blocks = rows // SEQ_MAX
    act = shape((rows, d), BF)
    return pl.pallas_call(
        self_forward_kernel,
        grid=(blocks,),
        in_specs=[row_block(d), whole(w), whole(bias), row_block(128), lead_block(HEAD_DIM)],
        out_specs=[row_block(d), row_block(d), row_block(d), col_block(d), lead_block(16)],
        out_shape=[act, act, act, shape((d, rows), BF), shape((blocks, 16, SEQ_MAX), F32)],
        scratch_shapes=[pltpu.VMEM((d, SEQ_MAX), BF)] * 2,
        compiler_params=params(("arbitrary",)),
        cost_estimate=cost(20e9, 12e6),
        name="self_forward",
    )(x, w, bias, kmark, qmark)


def cross_forward(x, mem, sot, wo, w, bias, gain, shift, kmark, qmark):
    rows, d = x.shape
    blocks = rows // SEQ_MAX
    act, wide = shape((rows, d), BF), shape((rows, d), F32)
    return pl.pallas_call(
        cross_forward_kernel,
        grid=(blocks,),
        in_specs=[
            row_block(d), row_block(d), col_block(d), whole(wo), whole(w), whole(bias), whole(gain), whole(shift),
            row_block(128), lead_block(HEAD_DIM),
        ],
        out_specs=[row_block(d)] * 5 + [col_block(d), lead_block(16), row_block(d)],
        out_shape=[wide, act, act, act, act, shape((d, rows), BF), shape((blocks, 16, SEQ_MAX), F32), wide],
        scratch_shapes=[pltpu.VMEM((d, SEQ_MAX), BF)] * 2,
        compiler_params=params(("arbitrary",)),
        cost_estimate=cost(24e9, 20e6),
        name="cross_forward",
    )(x, mem, sot, wo, w, bias, gain, shift, kmark, qmark)


def feed(second_sum, cot, win, bin_, wout, bout, gain, shift):
    rows, d = second_sum.shape
    ff = win.shape[1]
    width = 512
    chunks = ff // width
    fixed = lambda p, j: (0, 0)
    phase_chunk = lambda p, j: j * p
    return pl.pallas_call(
        feed_kernel,
        grid=(2, chunks),
        in_specs=[
            whole(second_sum), whole(cot),
            pl.BlockSpec((d, width), lambda p, j: (0, j)),
            pl.BlockSpec((1, width), lambda p, j: (0, j)),
            pl.BlockSpec((width, d), lambda p, j: (j, 0)),
            whole(bout), whole(gain), whole(shift),
        ],
        out_specs=[
            pl.BlockSpec((rows, d), fixed),
            pl.BlockSpec((rows, d), fixed),
            pl.BlockSpec((d, width), lambda p, j: (0, j * p)),
            pl.BlockSpec((width, d), lambda p, j: (j * p, 0)),
            pl.BlockSpec((1, width), lambda p, j: (0, j * p)),
            pl.BlockSpec((8, d), fixed),
        ],
        out_shape=[
            shape((rows, d), BF), shape((rows, d), F32), shape((d, ff), BF), shape((ff, d), BF),
            shape((1, ff), F32), shape((8, d), F32),
        ],
        scratch_shapes=[
            pltpu.VMEM((rows, d), BF), pltpu.VMEM((d, rows), BF),
            pltpu.VMEM((chunks, rows, width), BF), pltpu.VMEM((chunks, rows, width), F32),
            pltpu.VMEM((rows, d), F32), pltpu.VMEM((8, 128), F32), pltpu.VMEM((rows, d), BF),
        ],
        compiler_params=params(("arbitrary", "arbitrary")),
        cost_estimate=cost(40e9, 40e6),
        name="feed",
    )(second_sum, cot, win, bin_, wout, bout, gain, shift)


def back_scratch(d):
    return (
        [pltpu.VMEM((d, SEQ_MAX), BF)] * 2 + [pltpu.VMEM((SEQ_MAX, d), BF)] + [pltpu.VMEM((d, SEQ_MAX), BF)] * 2
        + [pltpu.VMEM((SEQ_MAX, d), BF)] * 2 + [pltpu.VMEM((4, d, d), F32), pltpu.VMEM((8, d), F32)]
    )


def cross_back(ssg, first_sum, low, mem, q, k, v, ot, lse, wo, w, gain, kmark, qmark):
    rows, d = low.shape
    blocks = rows // SEQ_MAX
    wide = shape((rows, d), F32)
    return pl.pallas_call(
        cross_back_kernel,
        grid=(blocks,),
        in_specs=[row_block(d)] * 7 + [
            col_block(d), lead_block(16), whole(wo), whole(w), whole(gain), row_block(128), lead_block(HEAD_DIM),
        ],
        out_specs=[
            row_block(d), row_block(d),
            pl.BlockSpec((4, d, d), lambda b: (0, 0, 0), pipeline_mode=pl.Buffered(1)),
            pl.BlockSpec((8, d), lambda b: (0, 0)),
        ],
        out_shape=[wide, wide, shape((4, d, d), BF), shape((8, d), F32)],
        scratch_shapes=back_scratch(d),
        compiler_params=params(("arbitrary",)),
        cost_estimate=cost(50e9, 30e6),
        name="cross_back",
    )(ssg, first_sum, low, mem, q, k, v, ot, lse, wo, w, gain, kmark, qmark)


def self_back(fsg, x, q, k, v, ot, lse, wo, w, kmark, qmark):
    rows, d = x.shape
    blocks = rows // SEQ_MAX
    return pl.pallas_call(
        self_back_kernel,
        grid=(blocks,),
        in_specs=[row_block(d)] * 5 + [
            col_block(d), lead_block(16), whole(wo), whole(w), row_block(128), lead_block(HEAD_DIM),
        ],
        out_specs=[
            row_block(d),
            pl.BlockSpec((4, d, d), lambda b: (0, 0, 0), pipeline_mode=pl.Buffered(1)),
            pl.BlockSpec((8, d), lambda b: (0, 0)),
        ],
        out_shape=[shape((rows, d), F32), shape((4, d, d), BF), shape((8, d), F32)],
        scratch_shapes=back_scratch(d),
        compiler_params=params(("arbitrary",)),
        cost_estimate=cost(50e9, 30e6),
        name="self_back",
    )(fsg, x, q, k, v, ot, lse, wo, w, kmark, qmark)


def key_marks(seg):
    odd = (seg & 1)[:, None]
    lane = lax.broadcasted_iota(jnp.int32, (seg.shape[0], 128), 1) % HEAD_DIM
    return jnp.where(lane == 0, 1 - odd, jnp.where(lane == 1, odd, 0)).astype(BF)


def query_marks(seg):
    odd = (seg & 1).reshape(-1, 1, SEQ_MAX)
    row = lax.broadcasted_iota(jnp.int32, (odd.shape[0], HEAD_DIM, SEQ_MAX), 1)
    return jnp.where(row == 0, odd, jnp.where(row == 1, 1 - odd, 0)).astype(BF) * (-MASKED)


def layer(query, memory, query_seg, memory_seg, params_, cotangent):
    proj, out, bias, gain, shift, win, bin_, wout, bout = params_
    bias, gain, shift = bias.astype(F32), gain.astype(F32), shift.astype(F32)
    bin_, bout = bin_.astype(F32)[None], bout.astype(F32)[None]
    qmark = query_marks(query_seg)
    smark, cmark = key_marks(query_seg), key_marks(memory_seg)
    sq, sk, sv, sot, slse = self_forward(query, proj[0:3], bias, smark, qmark)
    first_sum, low, cq, ck, cv, cot_, clse, second_sum = cross_forward(
        query, memory, sot, out, proj[3:6], bias, gain, shift, cmark, qmark
    )
    mixed, ssg, dwin, dwout, dbin, small3 = feed(second_sum, cotangent, win, bin_, wout, bout, gain, shift)
    fsg, memory_grad, cdw, small2 = cross_back(
        ssg, first_sum, low, memory, cq, ck, cv, cot_, clse, out[1:2], proj[3:6], gain, cmark, qmark
    )
    query_grad, sdw, small1 = self_back(fsg, query, sq, sk, sv, sot, slse, out[0:1], proj[0:3], smark, qmark)
    bias_grad = jnp.stack([small1[0], small1[1], small1[2], small2[0], small2[1], small2[2]])
    gain_grad = jnp.stack([small2[3], small3[3], small3[0]])
    shift_grad = jnp.stack([small2[4], small3[4], small3[1]])
    return mixed, query_grad, memory_grad, sdw, cdw, bias_grad, gain_grad, shift_grad, dwin, dbin[0], dwout, small3[2]


BOTH = ("dp", "fsdp")


def body(
    query, memory, query_seg, memory_seg, attn_proj, attn_out, attn_bias, norm_gain, norm_bias, ffn_in, ffn_in_bias,
    ffn_out, ffn_out_bias, cotangent,
):
    gather = functools.partial(lax.all_gather, axis_name=BOTH, tiled=True)
    scatter = functools.partial(lax.psum_scatter, axis_name=BOTH, tiled=True)
    full = (
        gather(attn_proj, axis=1), gather(attn_out, axis=1), gather(attn_bias, axis=1), gather(norm_gain, axis=1),
        gather(norm_bias, axis=1), gather(ffn_in, axis=0), gather(ffn_in_bias, axis=0), gather(ffn_out, axis=0),
        gather(ffn_out_bias, axis=0),
    )
    mixed, query_grad, memory_grad, sdw, cdw, bias_g, gain_g, shift_g, dwin, dbin, dwout, dbout = layer(
        query, memory, query_seg, memory_seg, full, cotangent
    )
    dwin = scatter(dwin, scatter_dimension=0)
    dwout = scatter(dwout, scatter_dimension=0)
    cdw = scatter(cdw, scatter_dimension=1)
    sdw = scatter(sdw, scatter_dimension=1)
    proj_grad = jnp.concatenate([sdw[:3], cdw[:3]]).astype(F32)
    out_grad = jnp.concatenate([sdw[3:], cdw[3:]]).astype(F32)
    return (
        mixed, query_grad, memory_grad, proj_grad, out_grad,
        scatter(bias_g, scatter_dimension=1), scatter(gain_g, scatter_dimension=1), scatter(shift_g, scatter_dimension=1),
        dwin.astype(F32), scatter(dbin, scatter_dimension=0), dwout.astype(F32), scatter(dbout, scatter_dimension=0),
    )


def solution(mesh):
    rows, mid, flat, row1 = P(BOTH, None), P(None, BOTH, None), P(None, BOTH), P(BOTH)
    return jax.shard_map(
        body,
        mesh=mesh,
        in_specs=(rows, rows, row1, row1, mid, mid, flat, flat, flat, rows, row1, rows, row1, rows),
        out_specs=(rows, rows, rows, mid, mid, flat, flat, flat, rows, row1, rows, row1),
        check_vma=False,
    )
```

time: 1440 us -> 925 us (0.64)
  matrix products: 403 us -> 0 us
  Pallas kernels: 0 us -> 189 us
  local copies, waits for them, and re-layouts: 167 us -> 38.5 us
  waiting for transfers between devices: 494 us -> 386 us
  other arithmetic: 62.9 us -> 8.78 us
    dot_general x67 -> x0, matrix products: 362 us -> none  [the longest x15 128 us: project(): return jnp.dot(left, right, preferred_element_type=jnp.float32)]
    reduce_scatter x4 -> x2, waiting for transfers between devices: 491 us -> 220 us  [the longest x1 110 us: body(): dwin = scatter(dwin, scatter_dimension=0)]
    pallas_call x0 -> x5, Pallas kernels: none -> 189 us  [the longest x1 54.1 us: feed(): pl.pallas_call(feed_kernel, grid=(2, chunks), in_specs=[whole(second_sum)...]
    unnamed x8 -> x10, waiting for transfers between devices: 2.65 us -> 166 us
    while x83 -> x0, local copies, waits for them, and re-layouts: 54.8 us -> none  [the longest x11 31 us: attend(): result, log_total = lax.map(attend_block, items)]
    sub x4 -> x0, matrix products: 41.1 us -> none  [attend_block(): weights = jnp.exp(scores - peak)]
    another operation x20 -> x0, local copies, waits for them, and re-layouts: 31.3 us -> none  [the longest x1 17.5 us: body(): jnp.stack([weight_grad(query, self_query_grad), weight_grad(query, self_k...]
    reduce_sum x20 -> x0, other arithmetic: 27.5 us -> none  [the longest x4 10.3 us: attend_block(): total = jnp.sum(weights, axis=-1, keepdims=True)]
  transfers between devices with their start and end apart: 8 -> 8, of which waited for: 4 -> 4; matrix products, arithmetic and copies ran while one was open for 18% -> 4% of each run, Pallas kernels for 0% -> 5%
where the time goes in v1:
time: 925 us; the launch traced here: 917 us
  waiting for transfers between devices  386 us (42%)
  blocking collectives  280 us (30%)
  Pallas kernels  189 us (20%)
  local copies, waits for them, and re-layouts  38.5 us (4%)
  between operations  14.9 us (2%)
    unnamed x10, waiting for transfers between devices  166 us
    reduce_scatter x1, waiting for transfers between devices, body(): dwin = scatter(dwin, scatter_dimension=0)  110 us
    reduce_scatter x1, waiting for transfers between devices, body(): dwout = scatter(dwout, scatter_dimension=0)  109 us
    unnamed x2, blocking collectives  79.7 us
    all_gather x1, blocking collectives, body(): gather(attn_bias, axis=1)  70.4 us
    all_gather x1, blocking collectives, body(): gather(norm_bias, axis=1)  65.9 us
    all_gather x1, blocking collectives, body(): gather(norm_gain, axis=1)  64 us
    pallas_call x1, Pallas kernels, feed(): pl.pallas_call(feed_kernel, grid=(2, chunks), in_specs=[whole(second_sum)...  54.1 us
  transfers between devices with their start and end apart: 8, of which 4 were waited for; matrix products, arithmetic and copies ran while one was open for 4% of the time, Pallas kernels for 5%

profile of v1, /device:TPU:0, one launch (start us, length us, event | category | flops | bytes accessed | tf_op | source)
XLA Modules:
  0.0 917.3 jit_solution(18225250482703705655)
XLA Ops:
  10.7 70.4 %all-gather = bf16[32,24,6]{1,2,0:T(8,128)(2,1)S(1)} all-gather(bf16[1,24,6]{1,2,0:T(8,128)(2,1)} %bitcast.53), channel_id=1, replica_groups=mesh['dp'=4,'fsdp'=8] {'dp','fsdp'}, dimensions={0}, use_global_device_ids=true | all-gather | bytes 9504 | tf_op jit(solution)/shard_map/all_gather | solution.py:506
  82.1 64.0 %all-gather.1 = bf16[32,24,3]{1,2,0:T(4,128)(2,1)S(1)} all-gather(bf16[1,24,3]{1,2,0:T(4,128)(2,1)} %bitcast.54), channel_id=1, replica_groups=mesh['dp'=4,'fsdp'=8] {'dp','fsdp'}, dimensions={0}, use_global_device_ids=true | all-gather | bytes 4752 | tf_op jit(solution)/shard_map/all_gather | solution.py:506
  147.0 65.9 %all-gather.2 = bf16[32,24,3]{1,2,0:T(4,128)(2,1)S(1)} all-gather(bf16[1,24,3]{1,2,0:T(4,128)(2,1)} %bitcast.55), channel_id=1, replica_groups=mesh['dp'=4,'fsdp'=8] {'dp','fsdp'}, dimensions={0}, use_global_device_ids=true | all-gather | bytes 4752 | tf_op jit(solution)/shard_map/all_gather | solution.py:507
  215.4 37.2 %all-reduce.8 = (bf16[3072]{0:T(1024)(128)(2,1)S(1)}, bf16[768]{0:T(1024)(128)(2,1)S(1)}) all-reduce(bf16[3072]{0:T(1024)(128)(2,1)S(1)} %dynamic-update-slice, bf16[768]{0:T(1024)(128)(2,1)S(1)} %dynamic-update-slice.1), channel_id=1, replica_groups=mesh['dp'=4,'fsdp'=8] {'dp','fsdp'}, use_global_device_ids=true, to_apply=%add | all-reduce | flops 3840 | bytes 15360
  254.6 1.9 fusion.5
  256.5 3.2 fusion.8
  259.7 6.5 fusion.7
  266.3 21.2 %self_forward.1 = (bf16[1024,768]{1,0:T(8,128)(2,1)}, bf16[1024,768]{1,0:T(8,128)(2,1)}, bf16[1024,768]{1,0:T(8,128)(2,1)}, bf16[768,1024]{1,0:T(8,128)(2,1)}, f32[2,16,512]{2,1,0:T(8,128)}) custom-call(bf16[1024,768]{1,0:T(8,128)(2,1)} %x_ref.5, bf16[3,768,768]{2,1,0:T(8,128)(2,1)} %get-tuple-element.72.w_ref, f32[6,768]{1,0:T(8,128)} %bitcast.44, ...), custom_call_target="tpu_custom_call" | custom-call | flops 20000000000 | bytes 12000000 | tf_op jit(solution)/shard_map/self_forward/pallas_call | solution.py:338
  287.4 27.4 %cross_forward.1 = (f32[1024,768]{1,0:T(8,128)}, bf16[1024,768]{1,0:T(8,128)(2,1)}, bf16[1024,768]{1,0:T(8,128)(2,1)}, bf16[1024,768]{1,0:T(8,128)(2,1)}, bf16[1...) custom-call(bf16[1024,768]{1,0:T(8,128)(2,1)} %x_ref.5, ...), custom_call_target="tpu_custom_call" | custom-call | flops 24000000000 | bytes 20000000 | tf_op jit(solution)/shard_map/cross_forward/pallas_call | solution.py:355
  314.9 54.1 %feed.1 = (bf16[1024,768]{1,0:T(8,128)(2,1)}, f32[1024,768]{1,0:T(8,128)}, bf16[768,3072]{1,0:T(8,128)(2,1)}, bf16[3072,768]{1,0:T(8,128)(2,1)}, f32[1,3072]{1,0:T(1,128)}, /*index=5*/f32[8,768]{1,0:T(8,128)}) custom-call(f32[1024,768]{1,0:T(8,128)} %get-tuple-element.39.ss_ref, bf16[1024,768]{1,0:T(8,128)(2,1)} %cot_ref.1, ...), custom_call_target="tpu_custom_call" | custom-call | flops 40000000000 | bytes 40000000 | tf_op jit(solution)/shard_map/feed/pallas_call | solution.py:378
  369.0 43.2 %cross_back.1 = (f32[1024,768]{1,0:T(8,128)}, f32[1024,768]{1,0:T(8,128)}, bf16[4,768,768]{2,1,0:T(8,128)(2,1)}, f32[8,768]{1,0:T(8,128)}) custom-call(f32[1024,768]{1,0:T(8,128)} %get-tuple-element.41.ssg_ref, f32[1024,768]{1,0:T(8,128)} %get-tuple-element.42.fs_ref, bf16[1024,768]{1,0:T(8,128)(2,1)} %get-tuple-element.43.low_ref, ...), custom_call_target="tpu_custom_call" | custom-call | flops 49999998976 | bytes 30000000 | tf_op jit(solution)/shard_map/cross_back/pallas_call | solution.py:422
  412.3 42.6 %self_back.1 = (f32[1024,768]{1,0:T(8,128)}, bf16[4,768,768]{2,1,0:T(8,128)(2,1)}, f32[8,768]{1,0:T(8,128)}) custom-call(f32[1024,768]{1,0:T(8,128)} %get-tuple-element.49.fsg_ref, bf16[1024,768]{1,0:T(8,128)(2,1)} %x_ref.5, bf16[1024,768]{1,0:T(8,128)(2,1)} %get-tuple-element.50.q_ref, bf16[1024,768]{1,0:T(8,128)(2,1)} %get-tuple-element.51.k_ref, ...), custom_call_target="tpu_custom_call" | custom-call | flops 49999998976 | bytes 30000000 | tf_op jit(solution)/shard_map/self_back/pallas_call | solution.py:444
  454.9 6.0 copy.41
  460.9 3.3 copy.55
  464.3 6.0 copy.43
  470.3 3.2 copy.56
  475.2 42.5 %all-reduce.7 = (f32[6,768]{1,0:T(8,128)S(1)}, f32[3,768]{1,0:T(4,128)S(1)}, f32[3,768]{1,0:T(4,128)S(1)}, f32[3072]{0:T(1024)S(1)}, f32[768]{0:T(1024)S(1)}) all-reduce(f32[6,768]{1,0:T(8,128)S(1)} %pad_maximum_fusion, f32[3,768]{1,0:T(4,128)S(1)} %pad_maximum_fusion.1, ...), channel_id=4, replica_groups=mesh['dp'=4,'fsdp'=8] {'dp','fsdp'}, use_global_device_ids=true, to_apply=%region_2.3.clone | all-reduce | flops 13056 | bytes 104448
  520.8 51.2 %reduce-scatter.16.cloned.1.call-done = bf16[24,3072]{1,0:T(8,128)(2,1)} async-done(((bf16[768,3072]{1,0:T(8,128)(2,1)}), bf16[24,3072]{1,0:T(8,128)(2,1)}) %reduce-scatter.16.cloned.1.call-update) | async-done | bytes 147472
  573.1 111.3 %reduce-scatter.18.cloned.1.call-done = bf16[24,3072]{1,0:T(8,128)(2,1)} async-done(((bf16[768,3072]{1,0:T(8,128)(2,1)}), bf16[24,3072]{1,0:T(8,128)(2,1)}) %reduce-scatter.18.cloned.1.call-update) | async-done | bytes 147472
  684.4 1.0 reshape.57
  685.5 110.4 %reduce-scatter.12.cloned.1.call-done = bf16[24,3072]{1,0:T(8,128)(2,1)} async-done(((bf16[768,3072]{1,0:T(8,128)(2,1)}), bf16[24,3072]{1,0:T(8,128)(2,1)}) %reduce-scatter.12.cloned.1.call-update) | async-done | bytes 147472 | tf_op jit(solution)/shard_map/reduce_scatter | solution.py:513
  795.9 1.6 convert_element_type.40
  799.1 109.4 %reduce-scatter.14.cloned.1.call-done = bf16[96,768]{1,0:T(8,128)(2,1)} async-done(((bf16[3072,768]{1,0:T(8,128)(2,1)}), bf16[96,768]{1,0:T(8,128)(2,1)}) %reduce-scatter.14.cloned.1.call-update) | async-done | bytes 147472 | tf_op jit(solution)/shard_map/reduce_scatter | solution.py:514
  908.4 1.6 convert_element_type.41
  (71 shorter events, 17.3 us)
Async XLA Ops:
  7.2 249.3 %all-gather.10.cloned.1.call-start = ((), (), s32[]{:S(2)}) async-start(), calls=%async_computation.5 | async-start | bytes 2433024 | tf_op jit(solution)/shard_map/all_gather | solution.py:506
  7.9 251.8 %all-gather.8.cloned.1.call-start = ((), (), s32[]{:S(2)}) async-start(), calls=%async_computation.4 | async-start | bytes 7299072 | tf_op jit(solution)/shard_map/all_gather | solution.py:506
  8.7 306.2 %all-gather.12.cloned.1.call-start = ((), (), s32[]{:S(2)}) async-start(), calls=%async_computation.6 | async-start | bytes 4866048 | tf_op jit(solution)/shard_map/all_gather | solution.py:507
  9.4 305.5 %all-gather.14.cloned.1.call-start = ((), (), s32[]{:S(2)}) async-start(), calls=%async_computation.7 | async-start | bytes 4866048 | tf_op jit(solution)/shard_map/all_gather | solution.py:507
  10.0 562.0 %reduce-scatter.16.cloned.1.call-start = ((), (), s32[]{:S(2)}) async-start(), calls=%async_computation.10 | async-start | bytes 4866048
  464.2 220.1 %reduce-scatter.18.cloned.1.call-start = ((), (), s32[]{:S(2)}) async-start(), calls=%async_computation.11 | async-start | bytes 4866048
  473.4 322.5 %reduce-scatter.12.cloned.1.call-start = ((), (), s32[]{:S(2)}) async-start(), calls=%async_computation.8 | async-start | bytes 4866048 | tf_op jit(solution)/shard_map/reduce_scatter | solution.py:513
  474.2 0.8 copy-start.3
  474.2 0.8 copy-start
  474.2 0.8 copy-start.2
  474.2 0.9 copy-start.1
  474.2 434.2 %reduce-scatter.14.cloned.1.call-start = ((), (), s32[]{:S(2)}) async-start(), calls=%async_computation.9 | async-start | bytes 4866048 | tf_op jit(solution)/shard_map/reduce_scatter | solution.py:514
Sparse Core Ops, SparseCore 0:
  10.9 60.2 all-gather.9
  74.1 71.5 all-gather.7
  148.6 62.1 all-gather.11
  213.6 62.4 all-gather.13
  464.3 107.6 reduce-scatter.15
  578.2 106.0 reduce-scatter.17
  689.8 106.0 reduce-scatter.11
  802.3 106.0 reduce-scatter.13
